TPU v7x, 32 devices: a whole 2x2x4 slice. The times are simulated.
32 devices in a mesh: elem: 8 (over z, y), grp: 4 (over x, core).
Axes of the slice: x: 2, y: 2, z: 4, core: 2. Of those that a mesh axis runs over, the one named last changes fastest.
Arguments:
- basis_values: bfloat16 [8, 1024, 8192], P('elem', 'grp'), may hold values from -0.0625 to 0.0625
- basis_derivs: bfloat16 [8, 1024, 8192], P('elem', 'grp'), may hold values from -0.0625 to 0.0625
- potential: float32 [8, 8192], P('elem', 'grp'), may hold values from 0.5 to 2
- hop_blocks: bfloat16 [8, 4, 1024, 1024], P('elem', None, 'grp'), may hold values from -0.1875 to 0.1875
- coeffs: bfloat16 [8, 1024, 4096], P('elem', None, 'grp'), may hold values from -6 to 6
- counts: int32 [8], replicated, may hold values from 256 to 1024, as said below
- neighbours: int32 [8, 4], replicated, may hold values from 0 to 7, as said below
Outputs:
- applied_bands: float32 [8, 1024, 4096], P('elem', None, 'grp')
Inputs may be any that keep to these rules, and one draw needn't show every extreme that they name: `counts`: count of live basis functions of each element; some element has exactly 1024 and some exactly 256. `neighbours`: four distinct elements, none the element itself.
All inputs are finite; a program needn't handle non-finite values.
Results may differ from a plain program's by a relative error of at most 0.0022.
Values may be sent and summed in bfloat16 or wider, within the bound.
A program may use at most 192 MiB of HBM per device.

v0:
```python
import jax
import jax.numpy as jnp
from jax import lax
from jax.sharding import PartitionSpec as P


def local(basis_values, basis_derivs, potential, hop_blocks, coeffs, counts, neighbours):
    values_slab, derivs_slab = (
        lax.all_to_all(basis_values, "grp", split_axis=2, concat_axis=1, tiled=True),
        lax.all_to_all(basis_derivs, "grp", split_axis=2, concat_axis=1, tiled=True),
    )
    values_slab = values_slab[0]
    derivs_slab = derivs_slab[0]
    weighted = (potential[0][None, :] * values_slab.astype(jnp.float32)).astype(jnp.bfloat16)
    partial_value = 0.5 * jnp.einsum(
        "ip,jp->ij", derivs_slab, derivs_slab, preferred_element_type=jnp.float32
    )
    partial_value = partial_value + jnp.einsum(
        "ip,jp->ij", values_slab, weighted, preferred_element_type=jnp.float32
    )
    element = lax.axis_index("elem")
    width = coeffs.shape[1]
    row_ids = jnp.arange(width, dtype=jnp.int32)
    live_rows = row_ids < counts[element]
    own_coeffs = jnp.where(live_rows[:, None], coeffs[0], jnp.zeros_like(coeffs[0]))
    near_ids = neighbours[element]
    initial = jnp.zeros((near_ids.shape[0], width, coeffs.shape[2]), jnp.bfloat16)
    pieces = lax.all_gather(own_coeffs[None], "elem", axis=0, tiled=True)
    inside = (near_ids >= 0) & (near_ids < pieces.shape[0])
    clipped = jnp.clip(near_ids, 0, pieces.shape[0] - 1)
    picked = jnp.take(pieces, clipped, axis=0)
    near_coeffs = jnp.where(inside[:, None, None], picked, initial)
    assembled_low = lax.psum(partial_value, "grp").astype(jnp.bfloat16)
    applied = jnp.dot(assembled_low, own_coeffs, preferred_element_type=jnp.float32)
    applied = applied + jnp.einsum(
        "krm,kmb->rb",
        lax.all_gather(hop_blocks, "grp", axis=2, tiled=True)[0],
        near_coeffs,
        preferred_element_type=jnp.float32,
    )
    result = jnp.where(live_rows[:, None], applied, jnp.zeros_like(applied))
    return result[None]


def solution(mesh):
    placed = (
        P("elem", "grp", None),
        P("elem", "grp", None),
        P("elem", "grp"),
        P("elem", None, "grp", None),
        P("elem", None, "grp"),
        P(),
        P(),
    )
    return jax.shard_map(
        local, mesh=mesh, in_specs=placed, out_specs=P("elem", None, "grp"), check_vma=False
    )
```

profile of v0, /device:TPU:0, one launch (start us, length us, event | category | flops | bytes accessed | tf_op | source)
XLA Modules:
  0.0 408.7 jit_solution(54028810329281735)
XLA Ops:
  6.5 0.0 all-gather.3.cloned.1.call-start
  6.5 1.2 dynamic_slice.6
  7.8 0.6 iota_compare_fusion
  8.4 3.1 broadcast_select_fusion
  11.6 0.0 all-gather.3.cloned.1.call-update
  11.6 18.2 %copy.22 = bf16[1,256,8192]{1,0,2:T(2,128)(2,1)} copy(bf16[1,256,8192]{2,1,0:T(8,128)(2,1)} %param.7) | data formatting | bytes 8388608 | tf_op args[0]
  29.7 0.6 broadcast.117
  30.3 43.5 %reduce.6 = bf16[8192,256]{1,0:T(8,128)(2,1)} reduce(bf16[8192,1,256]{2,1,0:T(2,128)(2,1)} %bitcast.46, bf16[]{:T(256)} %broadcast.117), dimensions={1}, to_apply=%bitcast.37.reduce_sub_computation | reduce | bytes 8388610
  73.8 5.1 %reshape.87 = bf16[4,2,262144]{2,1,0:T(2,128)(2,1)} reshape(bf16[8192,256]{1,0:T(8,128)(2,1)} %reduce.6) | data formatting | bytes 8388608
  78.9 4.8 %all-to-all-start.1 = ((bf16[4,2,262144]{2,1,0:T(2,128)(2,1)}), bf16[4,2,262144]{2,1,0:T(2,128)(2,1)}, u32[]{:S(2)}, u32[]{:S(2)}) async-start(bf16[4,2,262144]{2,1,0:T(2,128)(2,1)} %reshape.87), calls=%async_computation.1 | async-start | bytes 8388608 | tf_op jit(solution)/shard_map/all_to_all | solution.py:9
  83.8 0.0 all-gather.5.cloned.1.call-start
  83.8 0.7 all-gather.5.cloned.1.call-update
  84.5 18.0 %copy.20 = bf16[1,256,8192]{1,0,2:T(2,128)(2,1)} copy(bf16[1,256,8192]{2,1,0:T(8,128)(2,1)} %param.8) | data formatting | bytes 8388608 | tf_op args[1]
  102.5 43.6 %reduce.5 = bf16[8192,256]{1,0:T(8,128)(2,1)} reduce(bf16[8192,1,256]{2,1,0:T(2,128)(2,1)} %bitcast.47, bf16[]{:T(256)} %broadcast.117), dimensions={1}, to_apply=%bitcast.35.reduce_sub_computation | reduce | bytes 8388610
  146.1 5.1 %reshape.85 = bf16[4,2,262144]{2,1,0:T(2,128)(2,1)} reshape(bf16[8192,256]{1,0:T(8,128)(2,1)} %reduce.5) | data formatting | bytes 8388608
  151.2 0.0 copy-start.4
  151.2 0.0 all-to-all-done.1
  151.2 5.2 %all-to-all-start = ((bf16[4,2,262144]{2,1,0:T(2,128)(2,1)}), bf16[4,2,262144]{2,1,0:T(2,128)(2,1)}, u32[]{:S(2)}, u32[]{:S(2)}) async-start(bf16[4,2,262144]{2,1,0:T(2,128)(2,1)} %reshape.85), calls=%async_computation | async-start | bytes 8388608 | tf_op jit(solution)/shard_map/all_to_all | solution.py:10
  156.3 0.0 copy-done.4
  156.3 0.2 clamp_reduce_fusion
  156.5 0.2 and_reduce_fusion
  156.8 7.4 %reshape.88 = bf16[8192,1,256]{2,1,0:T(2,128)(2,1)} reshape(bf16[4,2,262144]{2,1,0:T(2,128)(2,1)} %all-to-all-done.1) | data formatting | bytes 8388608
  164.2 6.1 %copy.33 = bf16[1,256,8192]{1,2,0:T(8,128)(2,1)} copy(bf16[1,256,8192]{1,0,2:T(2,128)(2,1)} %bitcast.48) | data formatting | bytes 8388608
  170.3 0.0 copy-start.3
  170.3 6.3 %copy.24 = bf16[1,4,256,2048]{3,2,1,0:T(8,128)(2,1)} copy(bf16[1,4,256,2048]{2,3,1,0:T(8,128)(2,1)} %bitcast.44) | data formatting | bytes 8388608 | tf_op jit(solution)/shard_map/all_to_all | solution.py:9
  176.6 0.0 copy-done.3
  176.6 4.9 %multiply_convert_fusion = bf16[1,4,256,2048]{2,3,1,0:T(8,128)(2,1)} fusion(bf16[1,4,256,2048]{2,3,1,0:T(8,128)(2,1)} %bitcast.45, f32[2048]{0:T(1024)S(1)} %bitcast.54), kind=kLoop, calls=%fused_computation.8 | loop fusion | flops 6291456 | bytes 8396800 | tf_op jit(solution)/shard_map/convert_element_type | solution.py:14
  181.6 6.4 %copy.23 = bf16[1,4,256,2048]{3,2,1,0:T(8,128)(2,1)} copy(bf16[1,4,256,2048]{2,3,1,0:T(8,128)(2,1)} %multiply_convert_fusion) | data formatting | bytes 8388608 | tf_op jit(solution)/shard_map/convert_element_type | solution.py:14
  187.9 17.2 %all-to-all-done = bf16[4,2,262144]{2,1,0:T(2,128)(2,1)} async-done(((bf16[4,2,262144]{2,1,0:T(2,128)(2,1)}), bf16[4,2,262144]{2,1,0:T(2,128)(2,1)}, u32[]{:S(2)}, u32[]{:S(2)}) %all-to-all-start) | async-done | bytes 4194336 | tf_op jit(solution)/shard_map/all_to_all | solution.py:10
  205.2 7.4 %reshape.86 = bf16[8192,1,256]{2,1,0:T(2,128)(2,1)} reshape(bf16[4,2,262144]{2,1,0:T(2,128)(2,1)} %all-to-all-done) | data formatting | bytes 8388608
  212.6 6.1 %copy.32 = bf16[1,256,8192]{1,2,0:T(8,128)(2,1)} copy(bf16[1,256,8192]{1,0,2:T(2,128)(2,1)} %bitcast.49) | data formatting | bytes 8388608
  218.7 6.3 %copy.21 = bf16[1,4,256,2048]{3,2,1,0:T(8,128)(2,1)} copy(bf16[1,4,256,2048]{2,3,1,0:T(8,128)(2,1)} %bitcast.50) | data formatting | bytes 8388608 | tf_op jit(solution)/shard_map/all_to_all | solution.py:10
  225.0 0.0 copy-start
  225.0 0.0 copy-start.1
  225.0 8.2 %fusion.24 = f32[1024,1024]{1,0:T(8,128)S(1)} fusion(bf16[1024,2048]{1,0:T(8,128)(2,1)} %bitcast.53), kind=kOutput, calls=%fused_computation.36 | convolution fusion | flops 4294967296 | bytes 8388608 | tf_op jit(solution)/shard_map/ip,jp->ij/dot_general | solution.py:15
  233.3 0.0 copy-done
  233.3 0.0 copy-done.1
  233.3 6.1 %bitcast_add_fusion.1 = f32[1024,1024]{1,0:T(8,128)} fusion(f32[1024,1024]{1,0:T(8,128)S(1)} %fusion.24, bf16[1024,2048]{1,0:T(8,128)(2,1)S(1)} %bitcast.52, bf16[1024,2048]{1,0:T(8,128)(2,1)S(1)} %bitcast.51), kind=kOutput, calls=%fused_computation.14 | convolution fusion | flops 4297064448 | bytes 16777216 | tf_op jit(solution)/shard_map/ip,jp->ij/dot_general | solution.py:18
  239.4 120.0 %all-reduce.1 = bf16[1024,1024]{1,0:T(8,128)(2,1)S(1)} all-reduce(f32[1024,1024]{1,0:T(8,128)} %bitcast_add_fusion.1), channel_id=1, replica_groups=mesh['elem'=8,'grp'=4] {'grp'}, use_global_device_ids=true, to_apply=%region_0.1 | all-reduce | flops 1048576 | bytes 6291456 | tf_op jit(solution)/shard_map/psum | solution.py:33
  359.4 0.0 all-gather.3.cloned.1.call-done
  359.4 11.6 %fusion.23 = (bf16[8,512,1024]{2,1,0:T(8,128)(2,1)}, bf16[8,512,1024]{2,1,0:T(8,128)(2,1)}) fusion(bf16[8,1024,1024]{2,1,0:T(8,128)(2,1)} %all-gather.3.cloned.1.call-done), kind=kLoop, calls=%fused_computation.35 | loop fusion | bytes 33554432 | tf_op jit(solution)/shard_map/jit(_take)/gather | solution.py:31
  371.0 6.1 %gather_fusion = bf16[4,512,1024]{2,1,0:T(8,128)(2,1)} fusion(bf16[8,512,1024]{2,1,0:T(8,128)(2,1)} %get-tuple-element.5, s32[1024]{0:T(1024)S(1)} %pad_clamp_fusion), kind=kCustom, calls=%fused_computation | custom fusion | bytes 8388624 | tf_op jit(solution)/shard_map/jit(_take)/gather | solution.py:31
  377.2 6.2 %gather_fusion.1 = bf16[4,512,1024]{2,1,0:T(8,128)(2,1)} fusion(bf16[8,512,1024]{2,1,0:T(8,128)(2,1)} %get-tuple-element.6, s32[1024]{0:T(1024)S(1)} %pad_clamp_fusion), kind=kCustom, calls=%fused_computation.1 | custom fusion | bytes 8388624 | tf_op jit(solution)/shard_map/jit(_take)/gather | solution.py:31
  383.4 0.0 all-gather.5.cloned.1.call-done
  383.4 0.0 copy-start.2
  383.4 14.0 %fusion.1 = f32[1024,1024,1]{0,1,2:T(8,128)S(1)} fusion(bf16[4,512,1024]{2,1,0:T(8,128)(2,1)} %gather_fusion.1, bf16[4,512,1024]{2,1,0:T(8,128)(2,1)} %gather_fusion, bf16[1,4,1024,1024]{3,2,1,0:T(8,128)(2,1)} %all-gather.5.cloned.1.call-done, pred[4]{0:T(512)(128)(4,1)S(1)} %compare_and_fusion, pred[4]{0:T(512)(128)(4,1)S(1)} %and_reduce_fusion), kind=kOutput, calls=%fused_computation.4 | convolution fusion | flops 8615100416 | bytes 20971528 | tf_op jit(solution)/shard_map/krm,kmb->rb/dot_general | solution.py:35
  397.4 0.0 copy-done.2
  397.4 4.4 %fusion.9 = f32[1,1024,1024]{2,1,0:T(8,128)} fusion(f32[1024,1024,1]{0,1,2:T(8,128)S(1)} %fusion.1, pred[1024]{0:T(1024)(128)(4,1)S(1)} %iota_compare_fusion, bf16[1,1024,1024]{2,1,0:T(8,128)(2,1)S(1)} %copy-done.2, bf16[1024,1024]{1,0:T(8,128)(2,1)S(1)} %all-reduce.1), kind=kOutput, calls=%fused_computation.13 | convolution fusion | flops 2150629376 | bytes 12583936 | tf_op jit(solution)/shard_map/dot_general | solution.py:34
  (3 shorter events, 0.0 us)
Async XLA Ops:
  6.5 352.9 %all-gather.3.cloned.1.call-start = ((), (), s32[]{:S(2)}) async-start(), calls=%async_computation.2 | async-start | bytes 18874368 | tf_op jit(solution)/shard_map/all_gather | solution.py:28
  78.9 72.2 %all-to-all-start.1 = ((bf16[4,2,262144]{2,1,0:T(2,128)(2,1)}), bf16[4,2,262144]{2,1,0:T(2,128)(2,1)}, u32[]{:S(2)}, u32[]{:S(2)}) async-start(bf16[4,2,262144]{2,1,0:T(2,128)(2,1)} %reshape.87), calls=%async_computation.1 | async-start | bytes 8388608 | tf_op jit(solution)/shard_map/all_to_all | solution.py:9
  83.8 299.6 %all-gather.5.cloned.1.call-start = ((), (), s32[]{:S(2)}) async-start(), calls=%async_computation.3 | async-start | bytes 10485760 | tf_op jit(solution)/shard_map/all_gather | solution.py:37
  151.2 5.2 %copy-start.4 = (s32[8,4]{0,1:T(4,128)S(1)}, s32[8,4]{0,1:T(4,128)}, u32[]{:S(2)}) copy-start(s32[8,4]{0,1:T(4,128)} %param.13) | copy-start | bytes 388
  151.2 54.0 %all-to-all-start = ((bf16[4,2,262144]{2,1,0:T(2,128)(2,1)}), bf16[4,2,262144]{2,1,0:T(2,128)(2,1)}, u32[]{:S(2)}, u32[]{:S(2)}) async-start(bf16[4,2,262144]{2,1,0:T(2,128)(2,1)} %reshape.85), calls=%async_computation | async-start | bytes 8388608 | tf_op jit(solution)/shard_map/all_to_all | solution.py:10
  170.3 6.3 %copy-start.3 = (f32[1,2048]{1,0:T(1,128)S(1)}, f32[1,2048]{1,0:T(1,128)}, u32[]{:S(2)}) copy-start(f32[1,2048]{1,0:T(1,128)} %param.9) | copy-start | bytes 24580
  225.0 8.3 %copy-start = (bf16[1,4,256,2048]{3,2,1,0:T(8,128)(2,1)S(1)}, bf16[1,4,256,2048]{3,2,1,0:T(8,128)(2,1)}, u32[]{:S(2)}) copy-start(bf16[1,4,256,2048]{3,2,1,0:T(8,128)(2,1)} %copy.24) | copy-start | bytes 12582916
  225.0 8.3 %copy-start.1 = (bf16[1,4,256,2048]{3,2,1,0:T(8,128)(2,1)S(1)}, bf16[1,4,256,2048]{3,2,1,0:T(8,128)(2,1)}, u32[]{:S(2)}) copy-start(bf16[1,4,256,2048]{3,2,1,0:T(8,128)(2,1)} %copy.23) | copy-start | bytes 12582916
  383.4 14.1 %copy-start.2 = (bf16[1,1024,1024]{2,1,0:T(8,128)(2,1)S(1)}, bf16[1,1024,1024]{2,1,0:T(8,128)(2,1)}, u32[]{:S(2)}) copy-start(bf16[1,1024,1024]{2,1,0:T(8,128)(2,1)} %param.11) | copy-start | bytes 6291460
Sparse Core Ops, SparseCore 0:
  11.7 230.3 all-gather.2
  243.6 98.6 all-gather.4
where the time goes:
time: 411 us; the launch traced here: 409 us
  blocking collectives  120 us (29%)
  local copies, waits for them, and re-layouts  118 us (29%)
  other arithmetic  96.2 us (23%)
  matrix products  32.8 us (8%)
  waiting for transfers between devices  18 us (4%)
  between operations  13.5 us (3%)
  starting transfers between devices  10 us (2%)
    psum x1, blocking collectives, local(): assembled_low = lax.psum(partial_value, 'grp').astype(jnp.bfloat16)  120 us
    unnamed x2, other arithmetic  87.1 us
    unnamed x19, local copies, waits for them, and re-layouts  74 us
    gather x3, local copies, waits for them, and re-layouts, local(): picked = jnp.take(pieces, clipped, axis=0)  24 us
    all_to_all x1, waiting for transfers between devices, local(): lax.all_to_all(basis_derivs, 'grp', split_axis=2, concat_axis=1, tiled=True)  17.2 us
    dot_general x1, matrix products, local(): jnp.einsum('krm,kmb->rb', lax.all_gather(hop_blocks, 'grp', axis=2, tiled...  14 us
    dot_general x1, matrix products, local(): jnp.einsum('ip,jp->ij', derivs_slab, derivs_slab, preferred_element_type=...  8.24 us
  transfers between devices with their start and end apart: 4, of which 1 were waited for; matrix products, arithmetic and copies ran while one was open for 55% of the time, Pallas kernels for 0%

commit v1 on v0

--- a/solution.py
+++ b/solution.py
@@ -1,6 +1,10 @@
+import functools
+
 import jax
 import jax.numpy as jnp
 from jax import lax
+from jax.experimental import pallas as pl
+from jax.experimental.pallas import tpu as pltpu
 from jax.sharding import PartitionSpec as P
 
 
@@ -42,6 +46,432 @@
     return result[None]
 
 
+NT = (((1,), (1,)), ((), ()))
+PIECES = 4
+CHUNKS = 6
+
+
+def exchange_kernel(
+    values, derivs, pot, hop, coeffs,
+    near, hop_all, diag, off,
+    vbuf, dbuf, vbuf2, dbuf2, potbuf, acc_d, acc_o, got_d, got_o, got_x, sum_o, low_d, low_o,
+    load_sem, pair_send, pair_recv, slab_send, slab_recv, pot_sem, red_send, red_recv,
+    diag_send, diag_recv, off_send, off_recv, hop_send, hop_recv,
+    right_send, left_send, y_send, near_recv,
+):
+    e = lax.axis_index("elem")
+    g = lax.axis_index("grp")
+    z, y = e // 2, e % 2
+    x, c = g // 2, g % 2
+    partner = {"grp": 2 * x + 1 - c}
+    across = {"grp": 2 * (1 - x) + c}
+    beyond = {"grp": 2 * (1 - x) + 1 - c}
+    y_dev = {"elem": 2 * z + 1 - y}
+    right = {"elem": e + 2}
+    left = {"elem": e - 2}
+    depth = 4
+    rows, width = coeffs.shape
+    part = rows * 9 // 64 // 16 * 16
+    n_rows, slab = vbuf.shape[1], vbuf.shape[2]
+    piece = slab // PIECES
+    other_slab = 2 * (1 - x) + c
+
+    def remote(src, dst, ss, rs, dev):
+        return pltpu.make_async_remote_copy(
+            src_ref=src, dst_ref=dst, send_sem=ss, recv_sem=rs,
+            device_id=dev, device_id_type=pl.DeviceIdType.MESH,
+        )
+
+    barrier = pltpu.get_barrier_semaphore()
+    for dev in (partner, across, beyond, y_dev):
+        pl.semaphore_signal(barrier, inc=1, device_id=dev, device_id_type=pl.DeviceIdType.MESH)
+
+    @pl.when(z < depth - 1)
+    def _():
+        pl.semaphore_signal(barrier, inc=1, device_id=right, device_id_type=pl.DeviceIdType.MESH)
+
+    @pl.when(z > 0)
+    def _():
+        pl.semaphore_signal(barrier, inc=1, device_id=left, device_id_type=pl.DeviceIdType.MESH)
+
+    pl.semaphore_wait(barrier, 4 + (z + depth - 2) // (depth - 1) + (2 * depth - 3 - z) // (depth - 1))
+
+    def points(which, start, size):
+        return pl.ds(pl.multiple_of(which * slab + start, 128), size)
+
+    def slab_copy(core, arr, k, mine):
+        src = (values, derivs)[arr].at[:, points(2 * (1 - x) + core, k * piece, piece)]
+        row = g if mine else 2 * (1 - x) + core
+        dst = (vbuf, dbuf)[arr].at[row, :, pl.ds(k * piece, piece)]
+        return remote(
+            src, dst, slab_send.at[core, arr, k],
+            slab_recv.at[c if mine else core, arr, k], {"grp": 2 * (1 - x) + core},
+        )
+
+    def pair_copy(which, arr, mine):
+        ref = (values, derivs)[arr]
+        their = 1 - c if mine else c
+        src = ref.at[:, points(2 * x + their if which == 0 else 2 * (1 - x) + their, 0, slab)]
+        if which == 0:
+            dst = (vbuf, dbuf)[arr].at[g if mine else 2 * x + 1 - c]
+        else:
+            dst = (vbuf2, dbuf2)[arr].at[c if mine else 1 - c]
+        return remote(src, dst, pair_send.at[which, arr], pair_recv.at[which, arr], partner)
+
+    def pot_copy():
+        return remote(pot, potbuf.at[1], pot_sem.at[0], pot_sem.at[1], across)
+
+    pot_copy().start()
+    for k in range(PIECES):
+        for arr in range(2):
+            for core in range(2):
+                slab_copy(core, arr, k, True).start()
+
+    def rows_of(k):
+        if k < CHUNKS:
+            return pl.ds(k * part, part)
+        return pl.ds(CHUNKS * part, rows - CHUNKS * part)
+
+    def near_copy(sems, src_e, k, dev, own=False):
+        src = coeffs.at[rows_of(k)] if own else near.at[src_e, rows_of(k)]
+        return remote(src, near.at[src_e, rows_of(k)], sems.at[src_e, k], near_recv.at[src_e, k], dev)
+
+    def to_right(src_e, k, act, own=False):
+        @pl.when(z < depth - 1)
+        def _():
+            act(near_copy(right_send, src_e, k, right, own))
+
+    def to_left(src_e, k, act, own=False):
+        @pl.when(z > 0)
+        def _():
+            act(near_copy(left_send, src_e, k, left, own))
+
+    def start(copy):
+        copy.start()
+
+    def wait_send(copy):
+        copy.wait_send()
+
+    near_copy(y_send, e, CHUNKS, y_dev, True).start()
+    for k in range(CHUNKS + 1):
+        to_right(e, k, start, True)
+        to_left(e, k, start, True)
+        if k < CHUNKS:
+            near_copy(y_send, e, k, y_dev, True).start()
+
+    loads = []
+
+    def load(src, dst):
+        copy = pltpu.make_async_copy(src, dst, load_sem.at[len(loads)])
+        copy.start()
+        loads.append(copy)
+
+    for arr in range(2):
+        for which in range(2):
+            pair_copy(which, arr, True).start()
+    for arr in range(2):
+        ref = (values, derivs)[arr]
+        load(ref.at[:, points(g, 0, slab)], (vbuf, dbuf)[arr].at[g])
+        load(ref.at[:, points(other_slab, 0, slab)], (vbuf2, dbuf2)[arr].at[c])
+    load(pot, potbuf.at[0])
+    load(coeffs, near.at[e])
+    load(hop, hop_all.at[:, g])
+    n_hop = hop.shape[0]
+
+    def hop_pair(mine):
+        return remote(
+            hop, hop_all.at[:, g if mine else 2 * x + 1 - c], hop_send.at[0], hop_recv.at[0], partner
+        )
+
+    def hop_across(k, mine):
+        return remote(
+            hop.at[k], hop_all.at[k, g if mine else 2 * (1 - x) + c],
+            hop_send.at[1 + k], hop_recv.at[1 + k], across,
+        )
+
+    def hop_relay(k, mine):
+        row = 2 * (1 - x) + (c if mine else 1 - c)
+        ref = hop_all.at[k, row]
+        return remote(ref, ref, hop_send.at[1 + n_hop + k], hop_recv.at[1 + n_hop + k], partner)
+
+    hop_pair(True).start()
+
+    def product(v_low, d_low, v_high, d_high, weight):
+        weighted = (weight * v_high.astype(jnp.float32)).astype(jnp.bfloat16)
+        out = 0.5 * lax.dot_general(d_low, d_high, NT, preferred_element_type=jnp.float32)
+        return out + lax.dot_general(v_low, weighted, NT, preferred_element_type=jnp.float32)
+
+    half = 2 * n_rows
+
+    def two(ref, first, cols):
+        return ref[pl.ds(first, 2), :, cols].reshape(half, piece)
+
+    def diag_product():
+        for copy in loads[:5]:
+            copy.wait()
+        for arr in range(2):
+            for which in range(2):
+                pair_copy(which, arr, False).wait_recv()
+        pot_copy().wait_recv()
+        acc_d[...] = jnp.zeros_like(acc_d)
+
+        @pl.loop(0, PIECES)
+        def _(k):
+            cols = pl.ds(pl.multiple_of(k * piece, 128), piece)
+            for vb, db, first, which in ((vbuf, dbuf, 2 * x, 0), (vbuf2, dbuf2, 0, 1)):
+                v = two(vb, first, cols)
+                d = two(db, first, cols)
+                acc_d[...] += product(v, d, v, d, potbuf[which, 0:1, cols]).reshape(acc_d.shape)
+
+        remote(acc_d.at[1 - c], got_d, red_send.at[0], red_recv.at[0], partner).start()
+
+    def diag_finish():
+        remote(acc_d.at[1 - c], got_d, red_send.at[0], red_recv.at[0], partner).wait_recv()
+        low_d[...] = (acc_d[c] + got_d[...]).astype(jnp.bfloat16)
+        load(low_d, diag.at[g])
+        remote(low_d, diag.at[g], diag_send.at[0], diag_recv.at[0], partner).start()
+        remote(low_d, diag.at[g], diag_send.at[1], diag_recv.at[1], across).start()
+
+    def diag_relay(mine):
+        ref = diag.at[2 * (1 - x) + (c if mine else 1 - c)]
+        return remote(ref, ref, diag_send.at[2], diag_recv.at[2], partner)
+
+    def diag_forward():
+        remote(low_d, diag.at[2 * (1 - x) + c], diag_send.at[1], diag_recv.at[1], across).wait_recv()
+        diag_relay(True).start()
+
+    def off_piece(k):
+        for arr in range(2):
+            for core in range(2):
+                slab_copy(core, arr, k, False).wait_recv()
+        cols = pl.ds(k * piece, piece)
+        term = product(
+            two(vbuf, 0, cols), two(dbuf, 0, cols), two(vbuf, 2, cols), two(dbuf, 2, cols),
+            potbuf[0, 0:1, cols],
+        ).reshape(acc_o.shape)
+        if k == 0:
+            acc_o[...] = term
+        else:
+            acc_o[...] += term
+        if k == PIECES - 2:
+            hop_across(0, True).start()
+            hop_across(1, True).start()
+        if k == PIECES - 1:
+            remote(acc_o.at[1 - c], got_o, red_send.at[1], red_recv.at[1], partner).start()
+
+    def off_sum():
+        remote(acc_o.at[1 - c], got_o, red_send.at[1], red_recv.at[1], partner).wait_recv()
+        sum_o[...] = acc_o[c] + got_o[...]
+        remote(sum_o, got_x, red_send.at[2], red_recv.at[2], across).start()
+        hop_across(2, True).start()
+        hop_across(3, True).start()
+
+    def off_finish():
+        remote(sum_o, got_x, red_send.at[2], red_recv.at[2], across).wait_recv()
+        low_o[...] = (sum_o[...] + got_x[...]).astype(jnp.bfloat16)
+        load(low_o, off.at[c])
+        remote(low_o, off.at[c], off_send, off_recv, partner).start()
+
+    def hop_forward(k):
+        hop_across(k, False).wait_recv()
+        hop_relay(k, True).start()
+
+    plan = {
+        (1, 0): [diag_product],
+        (1, 1): [diag_finish],
+        (1, 2): [functools.partial(off_piece, 0)],
+        (1, 5): [functools.partial(off_piece, 1)],
+        (2, 0): [diag_forward],
+        (2, 2): [functools.partial(off_piece, 2)],
+        (2, 5): [functools.partial(off_piece, 3)],
+        (3, 0): [off_sum],
+        (3, 2): [functools.partial(hop_forward, 0), off_finish],
+        (3, 3): [functools.partial(hop_forward, 1)],
+    }
+
+    nbr = 2 * z + 1 - y
+    near_copy(y_send, nbr, CHUNKS, y_dev).wait_recv()
+    to_right(nbr, CHUNKS, start)
+    to_left(nbr, CHUNKS, start)
+
+    for d in range(1, depth):
+        for k in range(CHUNKS):
+            @pl.when(z >= d)
+            def _():
+                near_copy(right_send, e - 2 * d, k, right).wait_recv()
+                to_right(e - 2 * d, k, start)
+                near_copy(y_send, e - 2 * d, k, y_dev).start()
+
+            @pl.when(z + d < depth)
+            def _():
+                near_copy(left_send, e + 2 * d, k, left).wait_recv()
+                to_left(e + 2 * d, k, start)
+                near_copy(y_send, e + 2 * d, k, y_dev).start()
+
+            for step in plan.get((d, k), ()):
+                step()
+        for base in (e, nbr):
+            @pl.when(z >= d)
+            def _():
+                near_copy(right_send, base - 2 * d, CHUNKS, right).wait_recv()
+                to_right(base - 2 * d, CHUNKS, start)
+
+            @pl.when(z + d < depth)
+            def _():
+                near_copy(left_send, base + 2 * d, CHUNKS, left).wait_recv()
+                to_left(base + 2 * d, CHUNKS, start)
+
+    hop_forward(2)
+    hop_forward(3)
+
+    hop_pair(False).wait_recv()
+    for k in range(n_hop):
+        hop_relay(k, False).wait_recv()
+    remote(low_d, diag.at[2 * x + 1 - c], diag_send.at[0], diag_recv.at[0], partner).wait_recv()
+    diag_relay(False).wait_recv()
+    remote(low_o, off.at[1 - c], off_send, off_recv, partner).wait_recv()
+
+    @pl.loop(0, depth)
+    def _(zz):
+        for k in range(CHUNKS):
+            near_copy(y_send, 2 * zz + 1 - y, k, y_dev).wait_recv()
+
+    for copy in loads[5:]:
+        copy.wait()
+    pot_copy().wait_send()
+    for arr in range(2):
+        for which in range(2):
+            pair_copy(which, arr, True).wait_send()
+        for core in range(2):
+            for k in range(PIECES):
+                slab_copy(core, arr, k, True).wait_send()
+    hop_pair(True).wait_send()
+    for k in range(n_hop):
+        hop_across(k, True).wait_send()
+        hop_relay(k, True).wait_send()
+    remote(acc_d.at[1 - c], got_d, red_send.at[0], red_recv.at[0], partner).wait_send()
+    remote(acc_o.at[1 - c], got_o, red_send.at[1], red_recv.at[1], partner).wait_send()
+    remote(sum_o, got_x, red_send.at[2], red_recv.at[2], across).wait_send()
+    remote(low_d, diag.at[g], diag_send.at[0], diag_recv.at[0], partner).wait_send()
+    remote(low_d, diag.at[g], diag_send.at[1], diag_recv.at[1], across).wait_send()
+    diag_relay(True).wait_send()
+    remote(low_o, off.at[c], off_send, off_recv, partner).wait_send()
+    near_copy(y_send, e, CHUNKS, y_dev).wait_send()
+
+    @pl.loop(0, depth)
+    def _(zz):
+        src = 2 * zz + y
+        for k in range(CHUNKS):
+            near_copy(y_send, src, k, y_dev).wait_send()
+
+        @pl.when(zz <= z)
+        def _():
+            for k in range(CHUNKS + 1):
+                to_right(src, k, wait_send)
+            to_right(2 * zz + 1 - y, CHUNKS, wait_send)
+
+        @pl.when(zz >= z)
+        def _():
+            for k in range(CHUNKS + 1):
+                to_left(src, k, wait_send)
+            to_left(2 * zz + 1 - y, CHUNKS, wait_send)
+
+
+def apply_kernel(ids, live, blocks_a, blocks_h, near, out):
+    step = pl.program_id(0)
+    rows = lax.broadcasted_iota(jnp.int32, near.shape, 0)
+    picked = jnp.where(rows < live[step], near[...], jnp.zeros_like(near))
+
+    @pl.when(step == 0)
+    def _():
+        out[...] = jnp.dot(blocks_a[...], picked, preferred_element_type=jnp.float32)
+
+    @pl.when(step > 0)
+    def _():
+        out[...] += jnp.dot(blocks_h[...], picked, preferred_element_type=jnp.float32)
+
+    @pl.when(step == pl.num_programs(0) - 1)
+    def _():
+        ids_out = lax.broadcasted_iota(jnp.int32, out.shape, 0)
+        out[...] = jnp.where(ids_out < live[0], out[...], 0.0)
+
+
+def local_kernels(basis_values, basis_derivs, potential, hop_blocks, coeffs, counts, neighbours):
+    n_elem = counts.shape[0]
+    width, bands = coeffs.shape[1:]
+    n_rows, n_points = basis_values.shape[1:]
+    slab = potential.shape[1]
+    n_hop = hop_blocks.shape[1]
+    n_grp = width // n_rows
+    half = 2 * n_rows
+    bf16, f32 = jnp.bfloat16, jnp.float32
+    anywhere = pl.BlockSpec(memory_space=pl.ANY)
+    dma = pltpu.SemaphoreType.DMA
+    vmem = pltpu.VMEM
+    flops = 2 * half * half * 3 * 2 * slab
+    near, hop_all, diag, off = pl.pallas_call(
+        exchange_kernel,
+        out_shape=(
+            jax.ShapeDtypeStruct((n_elem, width, bands), bf16),
+            jax.ShapeDtypeStruct((n_hop, n_grp, n_rows, width), bf16),
+            jax.ShapeDtypeStruct((n_grp, n_rows, half), bf16),
+            jax.ShapeDtypeStruct((2, n_rows, half), bf16),
+        ),
+        in_specs=[anywhere] * 5,
+        out_specs=(anywhere,) * 4,
+        scratch_shapes=[
+            vmem((n_grp, n_rows, slab), bf16), vmem((n_grp, n_rows, slab), bf16),
+            vmem((2, n_rows, slab), bf16), vmem((2, n_rows, slab), bf16),
+            vmem((2, 8, slab), f32),
+            vmem((2, n_rows, half), f32), vmem((2, n_rows, half), f32),
+            vmem((n_rows, half), f32), vmem((n_rows, half), f32),
+            vmem((n_rows, half), f32), vmem((n_rows, half), f32),
+            vmem((n_rows, half), bf16), vmem((n_rows, half), bf16),
+            dma((9,)), dma((2, 2)), dma((2, 2)), dma((2, 2, PIECES)), dma((2, 2, PIECES)), dma((2,)),
+            dma((3,)), dma((3,)), dma((3,)), dma((3,)), dma, dma,
+            dma((1 + 2 * n_hop,)), dma((1 + 2 * n_hop,)),
+            dma((n_elem, CHUNKS + 1)), dma((n_elem, CHUNKS + 1)),
+            dma((n_elem, CHUNKS + 1)), dma((n_elem, CHUNKS + 1)),
+        ],
+        compiler_params=pltpu.CompilerParams(
+            collective_id=0, has_side_effects=True, vmem_limit_bytes=50 * 2 ** 20
+        ),
+        cost_estimate=pl.CostEstimate(flops=flops, bytes_accessed=2 ** 26, transcendentals=0),
+        name="exchange",
+    )(
+        basis_values[0], basis_derivs[0], jnp.broadcast_to(potential, (8, slab)),
+        hop_blocks[0], coeffs[0],
+    )
+    off = off.reshape(half, half)
+    diag = diag.reshape(2, half, half)
+    assembled = jnp.concatenate(
+        [jnp.concatenate([diag[0], off], 1), jnp.concatenate([off.T, diag[1]], 1)], 0
+    )
+    element = lax.axis_index("elem")
+    ids = jnp.concatenate([element[None].astype(jnp.int32), neighbours[element]])
+    live = counts[ids]
+    out = pl.pallas_call(
+        apply_kernel,
+        out_shape=jax.ShapeDtypeStruct((width, bands), f32),
+        grid_spec=pltpu.PrefetchScalarGridSpec(
+            num_scalar_prefetch=2,
+            grid=(1 + n_hop,),
+            in_specs=[
+                pl.BlockSpec((width, width), lambda s, ids, live: (0, 0)),
+                pl.BlockSpec((None, width, width), lambda s, ids, live: (jnp.maximum(s - 1, 0), 0, 0)),
+                pl.BlockSpec((None, width, bands), lambda s, ids, live: (ids[s], 0, 0)),
+            ],
+            out_specs=pl.BlockSpec((width, bands), lambda s, ids, live: (0, 0)),
+        ),
+        compiler_params=pltpu.CompilerParams(vmem_limit_bytes=50 * 2 ** 20),
+        cost_estimate=pl.CostEstimate(
+            flops=2 * (1 + n_hop) * width * width * bands, bytes_accessed=2 ** 25, transcendentals=0
+        ),
+        name="apply",
+    )(ids, live, assembled, hop_all.reshape(n_hop, width, width), near)
+    return out[None]
+
+
 def solution(mesh):
     placed = (
         P("elem", "grp", None),
@@ -52,6 +482,8 @@
         P(),
         P(),
     )
+    fits = mesh.shape["elem"] == 8 and mesh.shape["grp"] == 4
     return jax.shard_map(
-        local, mesh=mesh, in_specs=placed, out_specs=P("elem", None, "grp"), check_vma=False
-    )
+        local_kernels if fits else local,
+        mesh=mesh, in_specs=placed, out_specs=P("elem", None, "grp"), check_vma=False,
+    )

time: 411 us -> 201 us (0.49)
  Pallas kernels: 0 us -> 194 us
  blocking collectives: 120 us -> 0 us
  local copies, waits for them, and re-layouts: 118 us -> 6.7 us
  other arithmetic: 96.2 us -> 0.44 us
  matrix products: 32.8 us -> 0 us
  waiting for transfers between devices: 18 us -> 0 us
  between operations: 13.5 us -> 0.05 us
  starting transfers between devices: 10 us -> 0 us
    pallas_call x0 -> x2, Pallas kernels: none -> 194 us  [the longest x1 176 us: local_kernels(): pl.pallas_call(exchange_kernel, out_shape=(jax.ShapeDtypeStruct((n_elem,...]
    psum x1 -> x0, blocking collectives: 120 us -> none  [local(): assembled_low = lax.psum(partial_value, 'grp').astype(jnp.bfloat16)]
    unnamed x2 -> x0, other arithmetic: 87.1 us -> none
    unnamed x19 -> x6, local copies, waits for them, and re-layouts: 74 us -> 2.69 us
    dot_general x4 -> x0, matrix products: 32.8 us -> none  [the longest x1 14 us: local(): jnp.einsum('krm,kmb->rb', lax.all_gather(hop_blocks, 'grp', axis=2, tiled...]
    gather x3 -> x1, local copies, waits for them, and re-layouts: 24 us -> 1.3 us  [local_kernels(): live = counts[ids]]
    all_to_all x2 -> x0, waiting for transfers between devices: 17.3 us -> none  [the longest x1 17.2 us: local(): lax.all_to_all(basis_derivs, 'grp', split_axis=2, concat_axis=1, tiled=True)]
    all_to_all x2 -> x0, local copies, waits for them, and re-layouts: 12.6 us -> none  [the longest x1 6.34 us: local(): lax.all_to_all(basis_values, 'grp', split_axis=2, concat_axis=1, tiled=True)]
  transfers between devices with their start and end apart: 4 -> 0, of which waited for: 1 -> 0; matrix products, arithmetic and copies ran while one was open for 55% -> 0% of each run, Pallas kernels for 0% -> 0%
where the time goes in v1:
time: 201 us
  Pallas kernels  194 us (97%)
  local copies, waits for them, and re-layouts  6.7 us (3%)
    pallas_call x1, Pallas kernels, local_kernels(): pl.pallas_call(exchange_kernel, out_shape=(jax.ShapeDtypeStruct((n_elem,...  176 us
    pallas_call x1, Pallas kernels, local_kernels(): pl.pallas_call(apply_kernel, out_shape=jax.ShapeDtypeStruct((width, bands...  17.7 us

profile of v1, /device:TPU:0, one launch (start us, length us, event | category | flops | bytes accessed | tf_op | source)
XLA Modules:
  0.0 201.0 jit_solution(1082341245165119678)
XLA Ops:
  0.0 0.0 copy-start
  0.0 0.7 copy-done
  0.7 0.2 dynamic-slice_reduce_fusion
  0.9 0.1 fusion
  0.9 0.1 pad_add_fusion.ids
  1.0 1.3 gather_fusion
  2.3 0.7 broadcast_in_dim.16.pot
  3.0 0.0 copy-start.1
  3.0 1.6 copy-done.1
  4.6 176.0 %exchange.1 = (bf16[8,1024,1024]{2,1,0:T(8,128)(2,1)}, bf16[4,4,256,1024]{3,2,1,0:T(8,128)(2,1)}, bf16[4,256,512]{2,1,0:T(8,128)(2,1)S(1)}, bf16[2,256,512]{2,1,0:T(8,128)(2,1)S(1)}) custom-call(bf16[256,8192]{1,0:T(8,128)(2,1)} %bitcast.23, bf16[256,8192]{1,0:T(8,128)(2,1)} %bitcast.24, f32[8,2048]{1,0:T(8,128)S(1)} %broadcast_in_dim.16.pot, ...), custom_call_target="tpu_custom_call" | custom-call | flops 6442450944 | bytes 67108864 | tf_op jit(solution)/shard_map/exchange/pallas_call | solution.py:412
  180.7 0.2 copy.15
  180.9 0.9 fusion.1
  181.8 0.2 copy.14
  182.0 0.0 copy-start.2
  182.0 0.1 pad_maximum_fusion
  182.1 0.5 copy.13
  182.6 0.4 copy-done.2
  183.0 0.2 maximum_maximum_fusion.blocks_a
  183.2 17.7 %apply.1 = f32[1024,1024]{1,0:T(8,128)} custom-call(s32[5]{0:T(128)S(1)} %pad_add_fusion.ids, s32[5]{0:T(128)S(1)} %gather_fusion, bf16[1024,1024]{1,0:T(8,128)(2,1)S(1)} %maximum_maximum_fusion.blocks_a, bf16[4,1024,1024]{2,1,0:T(8,128)(2,1)} %bitcast.26, bf16[8,1024,1024]{2,1,0:T(8,128)(2,1)} %get-tuple-element.12.near), custom_call_target="tpu_custom_call" | custom-call | flops 10737418240 | bytes 33554432 | tf_op jit(solution)/shard_map/apply/pallas_call | solution.py:453
  (1 shorter events, 0.0 us)
Async XLA Ops:
  0.0 0.7 copy-start
  3.0 1.6 copy-start.1
  182.0 1.0 copy-start.2

commit v2 on v1

--- a/solution.py
+++ b/solution.py
@@ -51,13 +51,13 @@
 CHUNKS = 6
 
 
-def exchange_kernel(
-    values, derivs, pot, hop, coeffs,
-    near, hop_all, diag, off,
-    vbuf, dbuf, vbuf2, dbuf2, potbuf, acc_d, acc_o, got_d, got_o, got_x, sum_o, low_d, low_o,
+def hamiltonian_kernel(
+    values, derivs, pot, hop, coeffs, counts, neighbours, out,
+    near, hop_all, amat, acc,
+    vbuf, dbuf, vbuf2, dbuf2, potbuf, acc_d, acc_o, got_d, got_o, sum_o, low_o, got_x,
     load_sem, pair_send, pair_recv, slab_send, slab_recv, pot_sem, red_send, red_recv,
     diag_send, diag_recv, off_send, off_recv, hop_send, hop_recv,
-    right_send, left_send, y_send, near_recv,
+    right_send, left_send, y_send, near_recv, out_sem,
 ):
     e = lax.axis_index("elem")
     g = lax.axis_index("grp")
@@ -121,8 +121,7 @@
     def pot_copy():
         return remote(pot, potbuf.at[1], pot_sem.at[0], pot_sem.at[1], across)
 
-    pot_copy().start()
-    for k in range(PIECES):
+    def send_piece(k):
         for arr in range(2):
             for core in range(2):
                 slab_copy(core, arr, k, True).start()
@@ -152,6 +151,27 @@
     def wait_send(copy):
         copy.wait_send()
 
+    n_hop = hop.shape[0]
+
+    def hop_pair(mine):
+        return remote(
+            hop, hop_all.at[:, g if mine else 2 * x + 1 - c], hop_send.at[0], hop_recv.at[0], partner
+        )
+
+    def hop_across(k, mine):
+        return remote(
+            hop.at[k], hop_all.at[k, g if mine else 2 * (1 - x) + c],
+            hop_send.at[1 + k], hop_recv.at[1 + k], across,
+        )
+
+    def hop_relay(k, mine):
+        row = 2 * (1 - x) + (c if mine else 1 - c)
+        ref = hop_all.at[k, row]
+        return remote(ref, ref, hop_send.at[1 + n_hop + k], hop_recv.at[1 + n_hop + k], partner)
+
+    pot_copy().start()
+    for k in range(n_hop):
+        hop_across(k, True).start()
     near_copy(y_send, e, CHUNKS, y_dev, True).start()
     for k in range(CHUNKS + 1):
         to_right(e, k, start, True)
@@ -176,25 +196,9 @@
     load(pot, potbuf.at[0])
     load(coeffs, near.at[e])
     load(hop, hop_all.at[:, g])
-    n_hop = hop.shape[0]
-
-    def hop_pair(mine):
-        return remote(
-            hop, hop_all.at[:, g if mine else 2 * x + 1 - c], hop_send.at[0], hop_recv.at[0], partner
-        )
-
-    def hop_across(k, mine):
-        return remote(
-            hop.at[k], hop_all.at[k, g if mine else 2 * (1 - x) + c],
-            hop_send.at[1 + k], hop_recv.at[1 + k], across,
-        )
-
-    def hop_relay(k, mine):
-        row = 2 * (1 - x) + (c if mine else 1 - c)
-        ref = hop_all.at[k, row]
-        return remote(ref, ref, hop_send.at[1 + n_hop + k], hop_recv.at[1 + n_hop + k], partner)
-
     hop_pair(True).start()
+    send_piece(0)
+    acc[...] = jnp.zeros_like(acc)
 
     def product(v_low, d_low, v_high, d_high, weight):
         weighted = (weight * v_high.astype(jnp.float32)).astype(jnp.bfloat16)
@@ -221,24 +225,34 @@
             for vb, db, first, which in ((vbuf, dbuf, 2 * x, 0), (vbuf2, dbuf2, 0, 1)):
                 v = two(vb, first, cols)
                 d = two(db, first, cols)
-                acc_d[...] += product(v, d, v, d, potbuf[which, 0:1, cols]).reshape(acc_d.shape)
+                acc_d[...] += product(v, d, v, d, potbuf[which, :, cols]).reshape(acc_d.shape)
 
         remote(acc_d.at[1 - c], got_d, red_send.at[0], red_recv.at[0], partner).start()
+
+    def diag_block(row):
+        cols = pl.ds(pl.multiple_of(row // 2 * half, 128), half)
+        return amat.at[pl.ds(pl.multiple_of(row * n_rows, 16), n_rows), cols]
+
+    def diag_copy(row, which, dev):
+        ref = diag_block(row)
+        return remote(ref, ref, diag_send.at[which], diag_recv.at[which], dev)
 
     def diag_finish():
         remote(acc_d.at[1 - c], got_d, red_send.at[0], red_recv.at[0], partner).wait_recv()
-        low_d[...] = (acc_d[c] + got_d[...]).astype(jnp.bfloat16)
-        load(low_d, diag.at[g])
-        remote(low_d, diag.at[g], diag_send.at[0], diag_recv.at[0], partner).start()
-        remote(low_d, diag.at[g], diag_send.at[1], diag_recv.at[1], across).start()
+        diag_block(g)[...] = (acc_d[c] + got_d[...]).astype(jnp.bfloat16)
+        diag_copy(g, 0, partner).start()
+        diag_copy(g, 1, across).start()
 
     def diag_relay(mine):
-        ref = diag.at[2 * (1 - x) + (c if mine else 1 - c)]
-        return remote(ref, ref, diag_send.at[2], diag_recv.at[2], partner)
+        return diag_copy(2 * (1 - x) + (c if mine else 1 - c), 2, partner)
 
     def diag_forward():
-        remote(low_d, diag.at[2 * (1 - x) + c], diag_send.at[1], diag_recv.at[1], across).wait_recv()
+        diag_copy(2 * (1 - x) + c, 1, across).wait_recv()
         diag_relay(True).start()
+
+    def off_copy(row):
+        ref = amat.at[pl.ds(pl.multiple_of(row * n_rows, 16), n_rows), pl.ds(half, half)]
+        return remote(ref, ref, off_send, off_recv, partner)
 
     def off_piece(k):
         for arr in range(2):
@@ -247,46 +261,93 @@
         cols = pl.ds(k * piece, piece)
         term = product(
             two(vbuf, 0, cols), two(dbuf, 0, cols), two(vbuf, 2, cols), two(dbuf, 2, cols),
-            potbuf[0, 0:1, cols],
+            potbuf[0, :, cols],
         ).reshape(acc_o.shape)
         if k == 0:
             acc_o[...] = term
         else:
             acc_o[...] += term
-        if k == PIECES - 2:
-            hop_across(0, True).start()
-            hop_across(1, True).start()
         if k == PIECES - 1:
             remote(acc_o.at[1 - c], got_o, red_send.at[1], red_recv.at[1], partner).start()
 
     def off_sum():
         remote(acc_o.at[1 - c], got_o, red_send.at[1], red_recv.at[1], partner).wait_recv()
         sum_o[...] = acc_o[c] + got_o[...]
-        remote(sum_o, got_x, red_send.at[2], red_recv.at[2], across).start()
-        hop_across(2, True).start()
-        hop_across(3, True).start()
+        low_o[...] = sum_o[...].astype(jnp.bfloat16)
+        remote(low_o, got_x, red_send.at[2], red_recv.at[2], across).start()
 
     def off_finish():
-        remote(sum_o, got_x, red_send.at[2], red_recv.at[2], across).wait_recv()
-        low_o[...] = (sum_o[...] + got_x[...]).astype(jnp.bfloat16)
-        load(low_o, off.at[c])
-        remote(low_o, off.at[c], off_send, off_recv, partner).start()
+        remote(low_o, got_x, red_send.at[2], red_recv.at[2], across).wait_recv()
+        block = pl.ds(pl.multiple_of(c * n_rows, 16), n_rows)
+        total = sum_o[...] + got_x[...].astype(jnp.float32)
+        amat[block, pl.ds(half, half)] = total.astype(jnp.bfloat16)
+        off_copy(c).start()
 
     def hop_forward(k):
         hop_across(k, False).wait_recv()
         hop_relay(k, True).start()
 
+    def hop_ready():
+        hop_pair(False).wait_recv()
+        for k in range(n_hop):
+            hop_relay(k, False).wait_recv()
+        loads[5].wait()
+        loads[6].wait()
+
+    tile = 256
+
+    def apply(left_of, src_e, live):
+        @pl.loop(0, width // tile)
+        def _(n):
+            cols = pl.ds(pl.multiple_of(n * tile, tile), tile)
+            ids = lax.broadcasted_iota(jnp.int32, (rows, tile), 0)
+            block = near[src_e, :, cols]
+            masked = jnp.where(ids < live, block, jnp.zeros_like(block))
+            acc[:, cols] += jnp.dot(left_of(), masked, preferred_element_type=jnp.float32)
+
+    def apply_hop(src_e):
+        which, live = 0, 0
+        for k in range(n_hop):
+            same = neighbours[e, k] == src_e
+            which = jnp.where(same, k, which)
+            live = jnp.where(same, counts[src_e], live)
+        apply(lambda: hop_all[which].reshape(rows, rows), src_e, live)
+
+    def apply_column(d, own):
+        @pl.loop(0, 2 if d else 1)
+        def _(i):
+            shift = d * (1 - 2 * i)
+            src_e = 2 * (z + shift) + (y if own else 1 - y)
+
+            @pl.when((z + shift >= 0) & (z + shift < depth))
+            def _():
+                if not own:
+                    for k in range(CHUNKS):
+                        near_copy(y_send, src_e, k, y_dev).wait_recv()
+                apply_hop(src_e)
+
+    def apply_own():
+        diag_copy(2 * x + 1 - c, 0, partner).wait_recv()
+        diag_relay(False).wait_recv()
+        off_copy(1 - c).wait_recv()
+        amat[pl.ds(half, half), pl.ds(0, half)] = amat[pl.ds(0, half), pl.ds(half, half)].T
+        apply(lambda: amat[...], e, counts[e])
+
+    do = functools.partial
     plan = {
         (1, 0): [diag_product],
-        (1, 1): [diag_finish],
-        (1, 2): [functools.partial(off_piece, 0)],
-        (1, 5): [functools.partial(off_piece, 1)],
-        (2, 0): [diag_forward],
-        (2, 2): [functools.partial(off_piece, 2)],
-        (2, 5): [functools.partial(off_piece, 3)],
-        (3, 0): [off_sum],
-        (3, 2): [functools.partial(hop_forward, 0), off_finish],
-        (3, 3): [functools.partial(hop_forward, 1)],
+        (1, 1): [diag_finish, do(hop_forward, 0)],
+        (1, 2): [do(hop_forward, 1)],
+        (1, 3): [do(hop_forward, 2), do(send_piece, 1)],
+        (1, 5): [do(hop_forward, 3), diag_forward, do(send_piece, 2)],
+        (2, 1): [do(off_piece, 0), do(send_piece, 3)],
+        (2, 2): [hop_ready, do(apply_column, 0, False), do(apply_column, 1, True)],
+        (2, 4): [do(off_piece, 1)],
+        (3, 0): [do(off_piece, 2), do(apply_column, 1, False)],
+        (3, 2): [do(apply_column, 2, True)],
+        (3, 3): [do(off_piece, 3)],
+        (3, 4): [off_sum],
+        (3, 5): [off_finish, do(apply_column, 2, False)],
     }
 
     nbr = 2 * z + 1 - y
@@ -321,22 +382,19 @@
                 near_copy(left_send, base + 2 * d, CHUNKS, left).wait_recv()
                 to_left(base + 2 * d, CHUNKS, start)
 
-    hop_forward(2)
-    hop_forward(3)
-
-    hop_pair(False).wait_recv()
-    for k in range(n_hop):
-        hop_relay(k, False).wait_recv()
-    remote(low_d, diag.at[2 * x + 1 - c], diag_send.at[0], diag_recv.at[0], partner).wait_recv()
-    diag_relay(False).wait_recv()
-    remote(low_o, off.at[1 - c], off_send, off_recv, partner).wait_recv()
-
-    @pl.loop(0, depth)
-    def _(zz):
-        for k in range(CHUNKS):
-            near_copy(y_send, 2 * zz + 1 - y, k, y_dev).wait_recv()
-
-    for copy in loads[5:]:
+    apply_column(3, True)
+    apply_own()
+    apply_column(3, False)
+
+    copies = []
+    for t in range(rows // tile):
+        here = pl.ds(t * tile, tile)
+        ids = lax.broadcasted_iota(jnp.int32, (tile, width), 0) + t * tile
+        acc[here, :] = jnp.where(ids < counts[e], acc[here, :], 0.0)
+        copies.append(pltpu.make_async_copy(acc.at[here], out.at[here], out_sem.at[t]))
+        copies[-1].start()
+
+    for copy in copies:
         copy.wait()
     pot_copy().wait_send()
     for arr in range(2):
@@ -351,11 +409,11 @@
         hop_relay(k, True).wait_send()
     remote(acc_d.at[1 - c], got_d, red_send.at[0], red_recv.at[0], partner).wait_send()
     remote(acc_o.at[1 - c], got_o, red_send.at[1], red_recv.at[1], partner).wait_send()
-    remote(sum_o, got_x, red_send.at[2], red_recv.at[2], across).wait_send()
-    remote(low_d, diag.at[g], diag_send.at[0], diag_recv.at[0], partner).wait_send()
-    remote(low_d, diag.at[g], diag_send.at[1], diag_recv.at[1], across).wait_send()
+    remote(low_o, got_x, red_send.at[2], red_recv.at[2], across).wait_send()
+    diag_copy(g, 0, partner).wait_send()
+    diag_copy(g, 1, across).wait_send()
     diag_relay(True).wait_send()
-    remote(low_o, off.at[c], off_send, off_recv, partner).wait_send()
+    off_copy(c).wait_send()
     near_copy(y_send, e, CHUNKS, y_dev).wait_send()
 
     @pl.loop(0, depth)
@@ -375,25 +433,6 @@
             for k in range(CHUNKS + 1):
                 to_left(src, k, wait_send)
             to_left(2 * zz + 1 - y, CHUNKS, wait_send)
-
-
-def apply_kernel(ids, live, blocks_a, blocks_h, near, out):
-    step = pl.program_id(0)
-    rows = lax.broadcasted_iota(jnp.int32, near.shape, 0)
-    picked = jnp.where(rows < live[step], near[...], jnp.zeros_like(near))
-
-    @pl.when(step == 0)
-    def _():
-        out[...] = jnp.dot(blocks_a[...], picked, preferred_element_type=jnp.float32)
-
-    @pl.when(step > 0)
-    def _():
-        out[...] += jnp.dot(blocks_h[...], picked, preferred_element_type=jnp.float32)
-
-    @pl.when(step == pl.num_programs(0) - 1)
-    def _():
-        ids_out = lax.broadcasted_iota(jnp.int32, out.shape, 0)
-        out[...] = jnp.where(ids_out < live[0], out[...], 0.0)
 
 
 def local_kernels(basis_values, basis_derivs, potential, hop_blocks, coeffs, counts, neighbours):
@@ -409,66 +448,37 @@
     dma = pltpu.SemaphoreType.DMA
     vmem = pltpu.VMEM
     flops = 2 * half * half * 3 * 2 * slab
-    near, hop_all, diag, off = pl.pallas_call(
-        exchange_kernel,
-        out_shape=(
-            jax.ShapeDtypeStruct((n_elem, width, bands), bf16),
-            jax.ShapeDtypeStruct((n_hop, n_grp, n_rows, width), bf16),
-            jax.ShapeDtypeStruct((n_grp, n_rows, half), bf16),
-            jax.ShapeDtypeStruct((2, n_rows, half), bf16),
-        ),
-        in_specs=[anywhere] * 5,
-        out_specs=(anywhere,) * 4,
+    smem = pl.BlockSpec(memory_space=pltpu.SMEM)
+    out = pl.pallas_call(
+        hamiltonian_kernel,
+        out_shape=jax.ShapeDtypeStruct((width, bands), f32),
+        in_specs=[anywhere] * 5 + [smem] * 2,
+        out_specs=anywhere,
         scratch_shapes=[
+            vmem((n_elem, width, bands), bf16), vmem((n_hop, n_grp, n_rows, width), bf16),
+            vmem((width, width), bf16), vmem((width, bands), f32),
             vmem((n_grp, n_rows, slab), bf16), vmem((n_grp, n_rows, slab), bf16),
             vmem((2, n_rows, slab), bf16), vmem((2, n_rows, slab), bf16),
-            vmem((2, 8, slab), f32),
+            vmem((2, 1, slab), f32),
             vmem((2, n_rows, half), f32), vmem((2, n_rows, half), f32),
-            vmem((n_rows, half), f32), vmem((n_rows, half), f32),
-            vmem((n_rows, half), f32), vmem((n_rows, half), f32),
+            vmem((n_rows, half), f32), vmem((n_rows, half), f32), vmem((n_rows, half), f32),
             vmem((n_rows, half), bf16), vmem((n_rows, half), bf16),
-            dma((9,)), dma((2, 2)), dma((2, 2)), dma((2, 2, PIECES)), dma((2, 2, PIECES)), dma((2,)),
+            dma((7,)), dma((2, 2)), dma((2, 2)), dma((2, 2, PIECES)), dma((2, 2, PIECES)), dma((2,)),
             dma((3,)), dma((3,)), dma((3,)), dma((3,)), dma, dma,
             dma((1 + 2 * n_hop,)), dma((1 + 2 * n_hop,)),
             dma((n_elem, CHUNKS + 1)), dma((n_elem, CHUNKS + 1)),
-            dma((n_elem, CHUNKS + 1)), dma((n_elem, CHUNKS + 1)),
+            dma((n_elem, CHUNKS + 1)), dma((n_elem, CHUNKS + 1)), dma((4,)),
         ],
         compiler_params=pltpu.CompilerParams(
-            collective_id=0, has_side_effects=True, vmem_limit_bytes=50 * 2 ** 20
+            collective_id=0, has_side_effects=True, vmem_limit_bytes=60 * 2 ** 20
         ),
-        cost_estimate=pl.CostEstimate(flops=flops, bytes_accessed=2 ** 26, transcendentals=0),
-        name="exchange",
+        cost_estimate=pl.CostEstimate(
+            flops=flops + 2 * n_elem * width * width * bands, bytes_accessed=2 ** 25, transcendentals=0
+        ),
+        name="hamiltonian",
     )(
-        basis_values[0], basis_derivs[0], jnp.broadcast_to(potential, (8, slab)),
-        hop_blocks[0], coeffs[0],
-    )
-    off = off.reshape(half, half)
-    diag = diag.reshape(2, half, half)
-    assembled = jnp.concatenate(
-        [jnp.concatenate([diag[0], off], 1), jnp.concatenate([off.T, diag[1]], 1)], 0
-    )
-    element = lax.axis_index("elem")
-    ids = jnp.concatenate([element[None].astype(jnp.int32), neighbours[element]])
-    live = counts[ids]
-    out = pl.pallas_call(
-        apply_kernel,
-        out_shape=jax.ShapeDtypeStruct((width, bands), f32),
-        grid_spec=pltpu.PrefetchScalarGridSpec(
-            num_scalar_prefetch=2,
-            grid=(1 + n_hop,),
-            in_specs=[
-                pl.BlockSpec((width, width), lambda s, ids, live: (0, 0)),
-                pl.BlockSpec((None, width, width), lambda s, ids, live: (jnp.maximum(s - 1, 0), 0, 0)),
-                pl.BlockSpec((None, width, bands), lambda s, ids, live: (ids[s], 0, 0)),
-            ],
-            out_specs=pl.BlockSpec((width, bands), lambda s, ids, live: (0, 0)),
-        ),
-        compiler_params=pltpu.CompilerParams(vmem_limit_bytes=50 * 2 ** 20),
-        cost_estimate=pl.CostEstimate(
-            flops=2 * (1 + n_hop) * width * width * bands, bytes_accessed=2 ** 25, transcendentals=0
-        ),
-        name="apply",
-    )(ids, live, assembled, hop_all.reshape(n_hop, width, width), near)
+        basis_values[0], basis_derivs[0], potential, hop_blocks[0], coeffs[0], counts, neighbours
+    )
     return out[None]
 
 

time: 201 us -> 183 us (0.910)
  Pallas kernels: 194 us -> 176 us
    pallas_call x2 -> x1, Pallas kernels: 194 us -> 176 us  [local_kernels(): pl.pallas_call(hamiltonian_kernel, out_shape=jax.ShapeDtypeStruct((width,...]
    unnamed x6 -> x2, local copies, waits for them, and re-layouts: 2.69 us -> 6.14 us
where the time goes in v2:
time: 183 us; the launch traced here: 182 us
  Pallas kernels  176 us (96%)
  local copies, waits for them, and re-layouts  6.14 us (3%)
    pallas_call x1, Pallas kernels, local_kernels(): pl.pallas_call(hamiltonian_kernel, out_shape=jax.ShapeDtypeStruct((width,...  176 us
    unnamed x2, local copies, waits for them, and re-layouts  6.14 us

profile of v2, /device:TPU:0, one launch (start us, length us, event | category | flops | bytes accessed | tf_op | source)
XLA Modules:
  0.0 182.5 jit_solution(14289878535335986337)
XLA Ops:
  0.0 1.3 copy.8.neighbours
  1.3 176.3 %hamiltonian.1 = f32[1024,1024]{1,0:T(8,128)} custom-call(bf16[256,8192]{1,0:T(8,128)(2,1)} %bitcast.6, bf16[256,8192]{1,0:T(8,128)(2,1)} %bitcast.7, f32[1,2048]{1,0:T(1,128)} %pot.1, bf16[4,256,1024]{2,1,0:T(8,128)(2,1)} %bitcast.8, bf16[1024,1024]{1,0:T(8,128)(2,1)} %bitcast.9, s32[8]{0:T(128)} %counts.1, s32[8,4]{1,0:T(8,128)} %copy.8.neighbours), custom_call_target="tpu_custom_call" | custom-call | flops 23622320128 | bytes 33554432 | tf_op jit(solution)/shard_map/hamiltonian/pallas_call | solution.py:452
  177.7 4.8 %copy.10 = f32[1,1024,1024]{2,1,0:T(8,128)} copy(f32[1,1024,1024]{2,1,0:T(8,128)} %bitcast.5) | data formatting | bytes 8388608

commit v3 on v2

--- a/solution.py
+++ b/solution.py
@@ -52,7 +52,7 @@
 
 
 def hamiltonian_kernel(
-    values, derivs, pot, hop, coeffs, counts, neighbours, out,
+    values, derivs, pot, hop, coeffs, counts, neighbours, out, a_out,
     near, hop_all, amat, acc,
     vbuf, dbuf, vbuf2, dbuf2, potbuf, acc_d, acc_o, got_d, got_o, sum_o, low_o, got_x,
     load_sem, pair_send, pair_recv, slab_send, slab_recv, pot_sem, red_send, red_recv,
@@ -126,10 +126,14 @@
             for core in range(2):
                 slab_copy(core, arr, k, True).start()
 
+    first = CHUNKS * part - 16
+
     def rows_of(k):
-        if k < CHUNKS:
+        if k < CHUNKS - 1:
             return pl.ds(k * part, part)
-        return pl.ds(CHUNKS * part, rows - CHUNKS * part)
+        if k == CHUNKS - 1:
+            return pl.ds(k * part, first - k * part)
+        return pl.ds(first, rows - first)
 
     def near_copy(sems, src_e, k, dev, own=False):
         src = coeffs.at[rows_of(k)] if own else near.at[src_e, rows_of(k)]
@@ -295,6 +299,7 @@
         loads[6].wait()
 
     tile = 256
+    copies = []
 
     def apply(left_of, src_e, live):
         @pl.loop(0, width // tile)
@@ -308,7 +313,7 @@
     def apply_hop(src_e):
         which, live = 0, 0
         for k in range(n_hop):
-            same = neighbours[e, k] == src_e
+            same = neighbours[k, e] == src_e
             which = jnp.where(same, k, which)
             live = jnp.where(same, counts[src_e], live)
         apply(lambda: hop_all[which].reshape(rows, rows), src_e, live)
@@ -326,12 +331,13 @@
                         near_copy(y_send, src_e, k, y_dev).wait_recv()
                 apply_hop(src_e)
 
-    def apply_own():
+    def finish_own():
         diag_copy(2 * x + 1 - c, 0, partner).wait_recv()
         diag_relay(False).wait_recv()
         off_copy(1 - c).wait_recv()
         amat[pl.ds(half, half), pl.ds(0, half)] = amat[pl.ds(0, half), pl.ds(half, half)].T
-        apply(lambda: amat[...], e, counts[e])
+        copies.append(pltpu.make_async_copy(amat, a_out, out_sem.at[0]))
+        copies[-1].start()
 
     do = functools.partial
     plan = {
@@ -383,16 +389,11 @@
                 to_left(base + 2 * d, CHUNKS, start)
 
     apply_column(3, True)
-    apply_own()
+    finish_own()
     apply_column(3, False)
 
-    copies = []
-    for t in range(rows // tile):
-        here = pl.ds(t * tile, tile)
-        ids = lax.broadcasted_iota(jnp.int32, (tile, width), 0) + t * tile
-        acc[here, :] = jnp.where(ids < counts[e], acc[here, :], 0.0)
-        copies.append(pltpu.make_async_copy(acc.at[here], out.at[here], out_sem.at[t]))
-        copies[-1].start()
+    copies.append(pltpu.make_async_copy(acc, out, out_sem.at[1]))
+    copies[-1].start()
 
     for copy in copies:
         copy.wait()
@@ -435,6 +436,15 @@
             to_left(2 * zz + 1 - y, CHUNKS, wait_send)
 
 
+def own_kernel(counts, assembled, coeffs, hops, out):
+    live = counts[lax.axis_index("elem")]
+    ids = lax.broadcasted_iota(jnp.int32, coeffs.shape, 0)
+    masked = jnp.where(ids < live, coeffs[...], jnp.zeros_like(coeffs))
+    total = hops[...] + jnp.dot(assembled[...], masked, preferred_element_type=jnp.float32)
+    ids = lax.broadcasted_iota(jnp.int32, out.shape, 0)
+    out[...] = jnp.where(ids < live, total, 0.0)
+
+
 def local_kernels(basis_values, basis_derivs, potential, hop_blocks, coeffs, counts, neighbours):
     n_elem = counts.shape[0]
     width, bands = coeffs.shape[1:]
@@ -449,11 +459,13 @@
     vmem = pltpu.VMEM
     flops = 2 * half * half * 3 * 2 * slab
     smem = pl.BlockSpec(memory_space=pltpu.SMEM)
-    out = pl.pallas_call(
+    hops, assembled = pl.pallas_call(
         hamiltonian_kernel,
-        out_shape=jax.ShapeDtypeStruct((width, bands), f32),
+        out_shape=(
+            jax.ShapeDtypeStruct((width, bands), f32), jax.ShapeDtypeStruct((width, width), bf16),
+        ),
         in_specs=[anywhere] * 5 + [smem] * 2,
-        out_specs=anywhere,
+        out_specs=(anywhere, anywhere),
         scratch_shapes=[
             vmem((n_elem, width, bands), bf16), vmem((n_hop, n_grp, n_rows, width), bf16),
             vmem((width, width), bf16), vmem((width, bands), f32),
@@ -467,7 +479,7 @@
             dma((3,)), dma((3,)), dma((3,)), dma((3,)), dma, dma,
             dma((1 + 2 * n_hop,)), dma((1 + 2 * n_hop,)),
             dma((n_elem, CHUNKS + 1)), dma((n_elem, CHUNKS + 1)),
-            dma((n_elem, CHUNKS + 1)), dma((n_elem, CHUNKS + 1)), dma((4,)),
+            dma((n_elem, CHUNKS + 1)), dma((n_elem, CHUNKS + 1)), dma((2,)),
         ],
         compiler_params=pltpu.CompilerParams(
             collective_id=0, has_side_effects=True, vmem_limit_bytes=60 * 2 ** 20
@@ -477,8 +489,22 @@
         ),
         name="hamiltonian",
     )(
-        basis_values[0], basis_derivs[0], potential, hop_blocks[0], coeffs[0], counts, neighbours
-    )
+        basis_values[0], basis_derivs[0], potential, hop_blocks[0], coeffs[0], counts, neighbours.T
+    )
+    tile = 256
+    column = pl.BlockSpec((width, tile), lambda n: (0, n))
+    out = pl.pallas_call(
+        own_kernel,
+        out_shape=jax.ShapeDtypeStruct((width, bands), f32),
+        grid=(bands // tile,),
+        in_specs=[smem, pl.BlockSpec((width, width), lambda n: (0, 0)), column, column],
+        out_specs=column,
+        compiler_params=pltpu.CompilerParams(vmem_limit_bytes=60 * 2 ** 20),
+        cost_estimate=pl.CostEstimate(
+            flops=2 * width * width * bands, bytes_accessed=2 ** 24, transcendentals=0
+        ),
+        name="own",
+    )(counts, assembled, coeffs[0], hops)
     return out[None]
 
 

time: 183 us -> 183 us (level)
  Pallas kernels: 176 us -> 183 us
  local copies, waits for them, and re-layouts: 6.14 us -> 0 us
    pallas_call x1 -> x2, Pallas kernels: 176 us -> 183 us  [the longest x1 175 us: local_kernels(): pl.pallas_call(hamiltonian_kernel, out_shape=(jax.ShapeDtypeStruct((width...]
    unnamed x2 -> x0, local copies, waits for them, and re-layouts: 6.14 us -> none
where the time goes in v3:
time: 183 us
  Pallas kernels  183 us (100%)
    pallas_call x1, Pallas kernels, local_kernels(): pl.pallas_call(hamiltonian_kernel, out_shape=(jax.ShapeDtypeStruct((width...  175 us
    pallas_call x1, Pallas kernels, local_kernels(): pl.pallas_call(own_kernel, out_shape=jax.ShapeDtypeStruct((width, bands),...  7.4 us

profile of v3, /device:TPU:0, one launch (start us, length us, event | category | flops | bytes accessed | tf_op | source)
XLA Modules:
  0.0 182.8 jit_solution(7328756061334284517)
XLA Ops:
  0.0 175.4 %hamiltonian.1 = (f32[1024,1024]{1,0:T(8,128)}, bf16[1024,1024]{1,0:T(8,128)(2,1)}) custom-call(bf16[256,8192]{1,0:T(8,128)(2,1)} %bitcast.8, bf16[256,8192]{1,0:T(8,128)(2,1)} %bitcast.9, f32[1,2048]{1,0:T(1,128)} %pot.1, bf16[4,256,1024]{2,1,0:T(8,128)(2,1)} %bitcast.10, bf16[1024,1024]{1,0:T(8,128)(2,1)} %bitcast.6, s32[8]{0:T(128)} %counts.3, ...), custom_call_target="tpu_custom_call" | custom-call | flops 23622320128 | bytes 33554432 | tf_op jit(solution)/shard_map/hamiltonian/pallas_call | solution.py:462
  175.4 7.4 %own.1 = f32[1024,1024]{1,0:T(8,128)} custom-call(s32[8]{0:T(128)} %counts.3, bf16[1024,1024]{1,0:T(8,128)(2,1)} %get-tuple-element.7.assembled, bf16[1024,1024]{1,0:T(8,128)(2,1)} %bitcast.7, f32[1024,1024]{1,0:T(8,128)} %get-tuple-element.8.hops), custom_call_target="tpu_custom_call" | custom-call | flops 2147483648 | bytes 16777216 | tf_op jit(solution)/shard_map/own/pallas_call | solution.py:496

commit v4 on v2

--- a/solution.py
+++ b/solution.py
@@ -126,10 +126,14 @@
             for core in range(2):
                 slab_copy(core, arr, k, True).start()
 
+    first = CHUNKS * part - 16
+
     def rows_of(k):
-        if k < CHUNKS:
+        if k < CHUNKS - 1:
             return pl.ds(k * part, part)
-        return pl.ds(CHUNKS * part, rows - CHUNKS * part)
+        if k == CHUNKS - 1:
+            return pl.ds(k * part, first - k * part)
+        return pl.ds(first, rows - first)
 
     def near_copy(sems, src_e, k, dev, own=False):
         src = coeffs.at[rows_of(k)] if own else near.at[src_e, rows_of(k)]
@@ -296,22 +300,30 @@
 
     tile = 256
 
-    def apply(left_of, src_e, live):
+    def columns(n):
+        return pl.ds(pl.multiple_of(n * tile, tile), tile)
+
+    def add_product(n, left, src_e, live):
+        cols = columns(n)
+        ids = lax.broadcasted_iota(jnp.int32, (rows, tile), 0)
+        block = near[src_e, :, cols]
+        masked = jnp.where(ids < live, block, jnp.zeros_like(block))
+        acc[:, cols] += jnp.dot(left, masked, preferred_element_type=jnp.float32)
+
+    def choose(src_e):
+        which, live = 0, 0
+        for k in range(n_hop):
+            same = neighbours[k, e] == src_e
+            which = jnp.where(same, k, which)
+            live = jnp.where(same, counts[src_e], live)
+        return which, live
+
+    def apply_hop(src_e):
+        which, live = choose(src_e)
+
         @pl.loop(0, width // tile)
         def _(n):
-            cols = pl.ds(pl.multiple_of(n * tile, tile), tile)
-            ids = lax.broadcasted_iota(jnp.int32, (rows, tile), 0)
-            block = near[src_e, :, cols]
-            masked = jnp.where(ids < live, block, jnp.zeros_like(block))
-            acc[:, cols] += jnp.dot(left_of(), masked, preferred_element_type=jnp.float32)
-
-    def apply_hop(src_e):
-        which, live = 0, 0
-        for k in range(n_hop):
-            same = neighbours[e, k] == src_e
-            which = jnp.where(same, k, which)
-            live = jnp.where(same, counts[src_e], live)
-        apply(lambda: hop_all[which].reshape(rows, rows), src_e, live)
+            add_product(n, hop_all[which].reshape(rows, rows), src_e, live)
 
     def apply_column(d, own):
         @pl.loop(0, 2 if d else 1)
@@ -326,28 +338,53 @@
                         near_copy(y_send, src_e, k, y_dev).wait_recv()
                 apply_hop(src_e)
 
-    def apply_own():
+    def finish_own():
         diag_copy(2 * x + 1 - c, 0, partner).wait_recv()
         diag_relay(False).wait_recv()
         off_copy(1 - c).wait_recv()
         amat[pl.ds(half, half), pl.ds(0, half)] = amat[pl.ds(0, half), pl.ds(half, half)].T
-        apply(lambda: amat[...], e, counts[e])
+
+        @pl.loop(0, width // tile)
+        def _(n):
+            add_product(n, amat[...], e, counts[e])
+
+    def out_copy(n):
+        return pltpu.make_async_copy(acc.at[:, columns(n)], out.at[:, columns(n)], out_sem.at[n])
+
+    def finish():
+        at_end = (z == 0) | (z == depth - 1)
+        src_e = 2 * (depth - 1 - z) + 1 - y
+        which, live = choose(src_e)
+
+        @pl.when(at_end)
+        def _():
+            for k in range(CHUNKS):
+                near_copy(y_send, src_e, k, y_dev).wait_recv()
+
+        @pl.loop(0, width // tile)
+        def _(n):
+            @pl.when(at_end)
+            def _():
+                add_product(n, hop_all[which].reshape(rows, rows), src_e, live)
+
+            ids = lax.broadcasted_iota(jnp.int32, (rows, tile), 0)
+            acc[:, columns(n)] = jnp.where(ids < counts[e], acc[:, columns(n)], 0.0)
+            out_copy(n).start()
 
     do = functools.partial
     plan = {
         (1, 0): [diag_product],
-        (1, 1): [diag_finish, do(hop_forward, 0)],
-        (1, 2): [do(hop_forward, 1)],
-        (1, 3): [do(hop_forward, 2), do(send_piece, 1)],
-        (1, 5): [do(hop_forward, 3), diag_forward, do(send_piece, 2)],
-        (2, 1): [do(off_piece, 0), do(send_piece, 3)],
-        (2, 2): [hop_ready, do(apply_column, 0, False), do(apply_column, 1, True)],
-        (2, 4): [do(off_piece, 1)],
-        (3, 0): [do(off_piece, 2), do(apply_column, 1, False)],
-        (3, 2): [do(apply_column, 2, True)],
-        (3, 3): [do(off_piece, 3)],
-        (3, 4): [off_sum],
-        (3, 5): [off_finish, do(apply_column, 2, False)],
+        (1, 2): [diag_finish, do(hop_forward, 0)],
+        (1, 4): [do(hop_forward, 1), do(send_piece, 1)],
+        (1, 5): [do(hop_forward, 2)],
+        (2, 0): [do(hop_forward, 3), diag_forward, do(send_piece, 2)],
+        (2, 2): [hop_ready, do(apply_column, 0, False), do(send_piece, 3)],
+        (2, 3): [do(off_piece, 0)],
+        (2, 4): [do(apply_column, 1, True)],
+        (3, 0): [do(off_piece, 1), do(apply_column, 1, False)],
+        (3, 2): [do(off_piece, 2)],
+        (3, 3): [do(apply_column, 2, True)],
+        (3, 5): [do(off_piece, 3), off_sum, do(apply_column, 2, False), off_finish, finish_own],
     }
 
     nbr = 2 * z + 1 - y
@@ -383,19 +420,12 @@
                 to_left(base + 2 * d, CHUNKS, start)
 
     apply_column(3, True)
-    apply_own()
-    apply_column(3, False)
-
-    copies = []
-    for t in range(rows // tile):
-        here = pl.ds(t * tile, tile)
-        ids = lax.broadcasted_iota(jnp.int32, (tile, width), 0) + t * tile
-        acc[here, :] = jnp.where(ids < counts[e], acc[here, :], 0.0)
-        copies.append(pltpu.make_async_copy(acc.at[here], out.at[here], out_sem.at[t]))
-        copies[-1].start()
-
-    for copy in copies:
-        copy.wait()
+    finish()
+
+    @pl.loop(0, width // tile)
+    def _(n):
+        out_copy(n).wait()
+
     pot_copy().wait_send()
     for arr in range(2):
         for which in range(2):
@@ -467,7 +497,7 @@
             dma((3,)), dma((3,)), dma((3,)), dma((3,)), dma, dma,
             dma((1 + 2 * n_hop,)), dma((1 + 2 * n_hop,)),
             dma((n_elem, CHUNKS + 1)), dma((n_elem, CHUNKS + 1)),
-            dma((n_elem, CHUNKS + 1)), dma((n_elem, CHUNKS + 1)), dma((4,)),
+            dma((n_elem, CHUNKS + 1)), dma((n_elem, CHUNKS + 1)), dma((bands // 256,)),
         ],
         compiler_params=pltpu.CompilerParams(
             collective_id=0, has_side_effects=True, vmem_limit_bytes=60 * 2 ** 20
@@ -477,7 +507,7 @@
         ),
         name="hamiltonian",
     )(
-        basis_values[0], basis_derivs[0], potential, hop_blocks[0], coeffs[0], counts, neighbours
+        basis_values[0], basis_derivs[0], potential, hop_blocks[0], coeffs[0], counts, neighbours.T
     )
     return out[None]
 

time: 183 us -> 180 us (0.984)
    unnamed x2 -> x1, local copies, waits for them, and re-layouts: 6.14 us -> 4.79 us
where the time goes in v4:
time: 180 us
  Pallas kernels  175 us (97%)
  local copies, waits for them, and re-layouts  4.79 us (3%)
    pallas_call x1, Pallas kernels, local_kernels(): pl.pallas_call(hamiltonian_kernel, out_shape=jax.ShapeDtypeStruct((width,...  175 us
    unnamed x1, local copies, waits for them, and re-layouts  4.79 us

profile of v4, /device:TPU:0, one launch (start us, length us, event | category | flops | bytes accessed | tf_op | source)
XLA Modules:
  0.0 179.7 jit_solution(15157846321712421649)
XLA Ops:
  0.0 174.9 %hamiltonian.1 = f32[1024,1024]{1,0:T(8,128)} custom-call(bf16[256,8192]{1,0:T(8,128)(2,1)} %bitcast.7, bf16[256,8192]{1,0:T(8,128)(2,1)} %bitcast.8, f32[1,2048]{1,0:T(1,128)} %pot.1, bf16[4,256,1024]{2,1,0:T(8,128)(2,1)} %bitcast.9, bf16[1024,1024]{1,0:T(8,128)(2,1)} %bitcast.10, s32[8]{0:T(128)} %counts.1, s32[4,8]{1,0:T(4,128)} %bitcast.11), custom_call_target="tpu_custom_call" | custom-call | flops 23622320128 | bytes 33554432 | tf_op jit(solution)/shard_map/hamiltonian/pallas_call | solution.py:482
  174.9 4.8 %copy.9 = f32[1,1024,1024]{2,1,0:T(8,128)} copy(f32[1,1024,1024]{2,1,0:T(8,128)} %bitcast.6) | data formatting | bytes 8388608

commit v5 on v4

--- a/solution.py
+++ b/solution.py
@@ -202,6 +202,7 @@
     load(hop, hop_all.at[:, g])
     hop_pair(True).start()
     send_piece(0)
+    send_piece(1)
     acc[...] = jnp.zeros_like(acc)
 
     def product(v_low, d_low, v_high, d_high, weight):
@@ -253,10 +254,6 @@
     def diag_forward():
         diag_copy(2 * (1 - x) + c, 1, across).wait_recv()
         diag_relay(True).start()
-
-    def off_copy(row):
-        ref = amat.at[pl.ds(pl.multiple_of(row * n_rows, 16), n_rows), pl.ds(half, half)]
-        return remote(ref, ref, off_send, off_recv, partner)
 
     def off_piece(k):
         for arr in range(2):
@@ -272,20 +269,40 @@
         else:
             acc_o[...] += term
         if k == PIECES - 1:
-            remote(acc_o.at[1 - c], got_o, red_send.at[1], red_recv.at[1], partner).start()
+            for h in range(2):
+                core_copy(h).start()
+
+    halves = [pl.ds(h * (n_rows // 2), n_rows // 2) for h in range(2)]
+
+    def core_copy(h):
+        return remote(
+            acc_o.at[1 - c, halves[h]], got_o.at[halves[h]], red_send.at[1 + h], red_recv.at[1 + h], partner
+        )
+
+    def sum_copy(h):
+        return remote(
+            low_o.at[halves[h]], got_x.at[halves[h]], red_send.at[3 + h], red_recv.at[3 + h], across
+        )
+
+    def off_copy(row, h):
+        here = pl.ds(pl.multiple_of(row * n_rows + h * (n_rows // 2), 16), n_rows // 2)
+        ref = amat.at[here, pl.ds(half, half)]
+        return remote(ref, ref, off_send.at[h], off_recv.at[h], partner)
 
     def off_sum():
-        remote(acc_o.at[1 - c], got_o, red_send.at[1], red_recv.at[1], partner).wait_recv()
-        sum_o[...] = acc_o[c] + got_o[...]
-        low_o[...] = sum_o[...].astype(jnp.bfloat16)
-        remote(low_o, got_x, red_send.at[2], red_recv.at[2], across).start()
+        for h in range(2):
+            core_copy(h).wait_recv()
+            sum_o[halves[h]] = acc_o[c, halves[h]] + got_o[halves[h]]
+            low_o[halves[h]] = sum_o[halves[h]].astype(jnp.bfloat16)
+            sum_copy(h).start()
 
     def off_finish():
-        remote(low_o, got_x, red_send.at[2], red_recv.at[2], across).wait_recv()
-        block = pl.ds(pl.multiple_of(c * n_rows, 16), n_rows)
-        total = sum_o[...] + got_x[...].astype(jnp.float32)
-        amat[block, pl.ds(half, half)] = total.astype(jnp.bfloat16)
-        off_copy(c).start()
+        for h in range(2):
+            sum_copy(h).wait_recv()
+            here = pl.ds(pl.multiple_of(c * n_rows + h * (n_rows // 2), 16), n_rows // 2)
+            total = sum_o[halves[h]] + got_x[halves[h]].astype(jnp.float32)
+            amat[here, pl.ds(half, half)] = total.astype(jnp.bfloat16)
+            off_copy(c, h).start()
 
     def hop_forward(k):
         hop_across(k, False).wait_recv()
@@ -338,15 +355,28 @@
                         near_copy(y_send, src_e, k, y_dev).wait_recv()
                 apply_hop(src_e)
 
-    def finish_own():
+    low, high = pl.ds(0, half), pl.ds(half, half)
+
+    def add_blocks(row_blocks):
+        @pl.loop(0, width // tile)
+        def _(n):
+            cols = columns(n)
+            for here, there in row_blocks:
+                ids = lax.broadcasted_iota(jnp.int32, (half, tile), 0) + there.start
+                block = near[e, there, cols]
+                masked = jnp.where(ids < counts[e], block, jnp.zeros_like(block))
+                acc[here, cols] += jnp.dot(amat[here, there], masked, preferred_element_type=jnp.float32)
+
+    def apply_diag():
         diag_copy(2 * x + 1 - c, 0, partner).wait_recv()
         diag_relay(False).wait_recv()
-        off_copy(1 - c).wait_recv()
-        amat[pl.ds(half, half), pl.ds(0, half)] = amat[pl.ds(0, half), pl.ds(half, half)].T
-
-        @pl.loop(0, width // tile)
-        def _(n):
-            add_product(n, amat[...], e, counts[e])
+        add_blocks([(low, low), (high, high)])
+
+    def finish_own():
+        for h in range(2):
+            off_copy(1 - c, h).wait_recv()
+        amat[high, low] = amat[low, high].T
+        add_blocks([(low, high), (high, low)])
 
     def out_copy(n):
         return pltpu.make_async_copy(acc.at[:, columns(n)], out.at[:, columns(n)], out_sem.at[n])
@@ -374,17 +404,20 @@
     do = functools.partial
     plan = {
         (1, 0): [diag_product],
-        (1, 2): [diag_finish, do(hop_forward, 0)],
-        (1, 4): [do(hop_forward, 1), do(send_piece, 1)],
-        (1, 5): [do(hop_forward, 2)],
-        (2, 0): [do(hop_forward, 3), diag_forward, do(send_piece, 2)],
-        (2, 2): [hop_ready, do(apply_column, 0, False), do(send_piece, 3)],
+        (1, 2): [diag_finish, do(hop_forward, 0), do(send_piece, 2)],
+        (1, 4): [do(hop_forward, 1)],
+        (1, 5): [do(hop_forward, 2), do(send_piece, 3)],
+        (2, 0): [do(hop_forward, 3)],
+        (2, 2): [hop_ready, do(apply_column, 0, False)],
         (2, 3): [do(off_piece, 0)],
         (2, 4): [do(apply_column, 1, True)],
         (3, 0): [do(off_piece, 1), do(apply_column, 1, False)],
         (3, 2): [do(off_piece, 2)],
         (3, 3): [do(apply_column, 2, True)],
-        (3, 5): [do(off_piece, 3), off_sum, do(apply_column, 2, False), off_finish, finish_own],
+        (3, 5): [
+            do(off_piece, 3), off_sum, diag_forward, do(apply_column, 2, False), apply_diag, off_finish,
+            finish_own,
+        ],
     }
 
     nbr = 2 * z + 1 - y
@@ -438,12 +471,13 @@
         hop_across(k, True).wait_send()
         hop_relay(k, True).wait_send()
     remote(acc_d.at[1 - c], got_d, red_send.at[0], red_recv.at[0], partner).wait_send()
-    remote(acc_o.at[1 - c], got_o, red_send.at[1], red_recv.at[1], partner).wait_send()
-    remote(low_o, got_x, red_send.at[2], red_recv.at[2], across).wait_send()
+    for h in range(2):
+        core_copy(h).wait_send()
+        sum_copy(h).wait_send()
+        off_copy(c, h).wait_send()
     diag_copy(g, 0, partner).wait_send()
     diag_copy(g, 1, across).wait_send()
     diag_relay(True).wait_send()
-    off_copy(c).wait_send()
     near_copy(y_send, e, CHUNKS, y_dev).wait_send()
 
     @pl.loop(0, depth)
@@ -494,7 +528,7 @@
             vmem((n_rows, half), f32), vmem((n_rows, half), f32), vmem((n_rows, half), f32),
             vmem((n_rows, half), bf16), vmem((n_rows, half), bf16),
             dma((7,)), dma((2, 2)), dma((2, 2)), dma((2, 2, PIECES)), dma((2, 2, PIECES)), dma((2,)),
-            dma((3,)), dma((3,)), dma((3,)), dma((3,)), dma, dma,
+            dma((5,)), dma((5,)), dma((3,)), dma((3,)), dma((2,)), dma((2,)),
             dma((1 + 2 * n_hop,)), dma((1 + 2 * n_hop,)),
             dma((n_elem, CHUNKS + 1)), dma((n_elem, CHUNKS + 1)),
             dma((n_elem, CHUNKS + 1)), dma((n_elem, CHUNKS + 1)), dma((bands // 256,)),

time: 180 us -> 180 us (level)
  no operation moved by 1% of the time
where the time goes in v5:
time: 180 us
  Pallas kernels  175 us (97%)
  local copies, waits for them, and re-layouts  4.79 us (3%)
    pallas_call x1, Pallas kernels, local_kernels(): pl.pallas_call(hamiltonian_kernel, out_shape=jax.ShapeDtypeStruct((width,...  175 us
    unnamed x1, local copies, waits for them, and re-layouts  4.79 us

profile of v5, /device:TPU:0, one launch (start us, length us, event | category | flops | bytes accessed | tf_op | source)
XLA Modules:
  0.0 179.8 jit_solution(373667803692867720)
XLA Ops:
  0.0 175.0 %hamiltonian.1 = f32[1024,1024]{1,0:T(8,128)} custom-call(bf16[256,8192]{1,0:T(8,128)(2,1)} %bitcast.7, bf16[256,8192]{1,0:T(8,128)(2,1)} %bitcast.8, f32[1,2048]{1,0:T(1,128)} %pot.1, bf16[4,256,1024]{2,1,0:T(8,128)(2,1)} %bitcast.9, bf16[1024,1024]{1,0:T(8,128)(2,1)} %bitcast.10, s32[8]{0:T(128)} %counts.1, s32[4,8]{1,0:T(4,128)} %bitcast.11), custom_call_target="tpu_custom_call" | custom-call | flops 23622320128 | bytes 33554432 | tf_op jit(solution)/shard_map/hamiltonian/pallas_call | solution.py:516
  175.0 4.8 %copy.9 = f32[1,1024,1024]{2,1,0:T(8,128)} copy(f32[1,1024,1024]{2,1,0:T(8,128)} %bitcast.6) | data formatting | bytes 8388608

commit v6 on v4

--- a/solution.py
+++ b/solution.py
@@ -303,12 +303,12 @@
     def columns(n):
         return pl.ds(pl.multiple_of(n * tile, tile), tile)
 
-    def add_product(n, left, src_e, live):
+    def add_product(n, left, src_e, live, lo=0, hi=rows):
         cols = columns(n)
-        ids = lax.broadcasted_iota(jnp.int32, (rows, tile), 0)
-        block = near[src_e, :, cols]
+        ids = lax.broadcasted_iota(jnp.int32, (hi - lo, tile), 0) + lo
+        block = near[src_e, pl.ds(lo, hi - lo), cols]
         masked = jnp.where(ids < live, block, jnp.zeros_like(block))
-        acc[:, cols] += jnp.dot(left, masked, preferred_element_type=jnp.float32)
+        acc[:, cols] += jnp.dot(left[:, lo:hi], masked, preferred_element_type=jnp.float32)
 
     def choose(src_e):
         which, live = 0, 0
@@ -351,21 +351,35 @@
     def out_copy(n):
         return pltpu.make_async_copy(acc.at[:, columns(n)], out.at[:, columns(n)], out_sem.at[n])
 
-    def finish():
-        at_end = (z == 0) | (z == depth - 1)
-        src_e = 2 * (depth - 1 - z) + 1 - y
+    at_end = (z == 0) | (z == depth - 1)
+    far = [2 * (depth - 1 - z) + y, 2 * (depth - 1 - z) + 1 - y]
+    split = first // tile * tile
+
+    def add_far(n, src_e, lo, hi):
         which, live = choose(src_e)
-
+        add_product(n, hop_all[which].reshape(rows, rows), src_e, live, lo, hi)
+
+    def far_first():
         @pl.when(at_end)
         def _():
+            @pl.loop(0, width // tile)
+            def _(n):
+                add_far(n, far[0], 0, split)
+
             for k in range(CHUNKS):
-                near_copy(y_send, src_e, k, y_dev).wait_recv()
-
+                near_copy(y_send, far[1], k, y_dev).wait_recv()
+
+            @pl.loop(0, width // tile)
+            def _(n):
+                add_far(n, far[1], 0, split)
+
+    def finish():
         @pl.loop(0, width // tile)
         def _(n):
             @pl.when(at_end)
             def _():
-                add_product(n, hop_all[which].reshape(rows, rows), src_e, live)
+                for src_e in far:
+                    add_far(n, src_e, split, rows)
 
             ids = lax.broadcasted_iota(jnp.int32, (rows, tile), 0)
             acc[:, columns(n)] = jnp.where(ids < counts[e], acc[:, columns(n)], 0.0)
@@ -384,7 +398,7 @@
         (3, 0): [do(off_piece, 1), do(apply_column, 1, False)],
         (3, 2): [do(off_piece, 2)],
         (3, 3): [do(apply_column, 2, True)],
-        (3, 5): [do(off_piece, 3), off_sum, do(apply_column, 2, False), off_finish, finish_own],
+        (3, 5): [do(off_piece, 3), off_sum, do(apply_column, 2, False), off_finish, finish_own, far_first],
     }
 
     nbr = 2 * z + 1 - y
@@ -419,7 +433,6 @@
                 near_copy(left_send, base + 2 * d, CHUNKS, left).wait_recv()
                 to_left(base + 2 * d, CHUNKS, start)
 
-    apply_column(3, True)
     finish()
 
     @pl.loop(0, width // tile)

time: 180 us -> 180 us (level)
  no operation moved by 1% of the time
where the time goes in v6:
time: 180 us
  Pallas kernels  175 us (97%)
  local copies, waits for them, and re-layouts  4.79 us (3%)
    pallas_call x1, Pallas kernels, local_kernels(): pl.pallas_call(hamiltonian_kernel, out_shape=jax.ShapeDtypeStruct((width,...  175 us
    unnamed x1, local copies, waits for them, and re-layouts  4.79 us

profile of v6, /device:TPU:0, one launch (start us, length us, event | category | flops | bytes accessed | tf_op | source)
XLA Modules:
  0.0 179.6 jit_solution(9556710628788190144)
XLA Ops:
  0.0 174.8 %hamiltonian.1 = f32[1024,1024]{1,0:T(8,128)} custom-call(bf16[256,8192]{1,0:T(8,128)(2,1)} %bitcast.7, bf16[256,8192]{1,0:T(8,128)(2,1)} %bitcast.8, f32[1,2048]{1,0:T(1,128)} %pot.1, bf16[4,256,1024]{2,1,0:T(8,128)(2,1)} %bitcast.9, bf16[1024,1024]{1,0:T(8,128)(2,1)} %bitcast.10, s32[8]{0:T(128)} %counts.1, s32[4,8]{1,0:T(4,128)} %bitcast.11), custom_call_target="tpu_custom_call" | custom-call | flops 23622320128 | bytes 33554432 | tf_op jit(solution)/shard_map/hamiltonian/pallas_call | solution.py:495
  174.8 4.8 %copy.9 = f32[1,1024,1024]{2,1,0:T(8,128)} copy(f32[1,1024,1024]{2,1,0:T(8,128)} %bitcast.6) | data formatting | bytes 8388608
